TPU v7x, 32 devices: a whole 2x2x4 slice. The times are simulated.
32 devices in a mesh: row: 4 (over y, x), col: 8 (over z, core).
Axes of the slice: x: 2, y: 2, z: 4, core: 2. Of those that a mesh axis runs over, the one named last changes fastest.
Arguments:
- tiles: bfloat16 [256, 256, 256], P(('row', 'col')), may hold values from -0.09375 to 0.09375
- tile_rows: int32 [256], P(('row', 'col')), may hold values from 0 to 3, as said below
- tile_cols: int32 [256], P(('row', 'col')), may hold values from 0 to 1
- tile_count: int32 [32], P(('row', 'col')), may hold values from 0 to 8, as said below
- bounds: float32 [2], replicated, may hold values from -1 to 2, as said below
- vectors: float32 [4096, 128], P(('row', 'col')), may hold values from -6 to 6
Outputs:
- filtered: float32 [4096, 128], P(('row', 'col'))
- gram: float32 [128, 128], replicated
Inputs may be any that keep to these rules, and one draw needn't show every extreme that they name: `tile_rows`: within each device the first tile_count slots name distinct blocks with global block row I <= global block column J; the device's diagonal blocks (I = J) come first; every diagonal block of the Hamiltonian is stored; slots after the live ones hold valid indices but are not part of the matrix. `tile_count`: devices whose block rows all lie below their block columns have no live slot; some device has all 8 slots live. bounds[0] < -0.5 and bounds[1] > 1.0.
All inputs are finite; a program needn't handle non-finite values.
Results may differ from a plain program's by a relative error of at most 0.0037.
Values may be sent and summed in bfloat16 or wider, within the bound.
A program may use at most 64 MiB of HBM per device.

v0:
```python
import jax
import jax.numpy as jnp
from jax import lax
from jax.sharding import PartitionSpec as P

BLK_COL = 2


def spread(block, axis, holder):
    block = jnp.where(lax.axis_index(axis) == holder, block, jnp.zeros_like(block))
    return lax.psum(block, axis)


def on_device(tiles, tile_rows, tile_cols, tile_count, bounds, vectors):
    col_ratio = lax.axis_size("col") // lax.axis_size("row")
    col_index = lax.axis_index("col")
    row_index = lax.axis_index("row")
    root_row = col_index // col_ratio
    slot_total = tiles.shape[0]
    block_size = tiles.shape[1]
    share_rows = vectors.shape[0]
    width_vecs = vectors.shape[1]
    group_rows = share_rows * lax.axis_size("col")
    group_blocks = group_rows // block_size
    column_rows = BLK_COL * block_size
    total_rows = share_rows * lax.axis_size("row") * lax.axis_size("col")
    offset = col_index % col_ratio * column_rows
    live_mask = (jnp.arange(slot_total, dtype=jnp.int32) < tile_count[0]).astype(jnp.bfloat16)
    owner_flag = (row_index == root_row).astype(jnp.float32)
    center = (bounds[1] + bounds[0]) * 0.5
    halfwidth = (bounds[1] - bounds[0]) * 0.5

    def apply_hamiltonian(current_vec):
        vector_panel = current_vec.astype(jnp.bfloat16)
        row_panel = lax.all_gather(vector_panel, "col", axis=0, tiled=True)
        col_piece = lax.dynamic_slice_in_dim(row_panel, offset, column_rows, 0)
        col_panel = spread(col_piece, "row", root_row)
        row_input = row_panel.reshape(group_blocks, block_size, width_vecs)
        col_input = col_panel.reshape(BLK_COL, block_size, width_vecs)
        start_rows = jnp.zeros((group_blocks, block_size, width_vecs), jnp.float32)
        start_cols = jnp.zeros((BLK_COL, block_size, width_vecs), jnp.float32)
        masked_cols = col_input[tile_cols] * live_mask[:, None, None]
        masked_rows = row_input[tile_rows] * live_mask[:, None, None]
        forward = jnp.einsum("tab,tbk->tak", tiles, masked_cols, preferred_element_type=jnp.float32)
        backward = jnp.einsum(
            "tab,tak->tbk", tiles, masked_rows, preferred_element_type=jnp.float32
        )
        row_part = start_rows.at[tile_rows].add(forward)
        col_part = start_cols.at[tile_cols].add(backward)
        column_total = lax.psum(col_part, "row")
        row_part = row_part.reshape(group_rows, width_vecs)
        present = lax.dynamic_slice_in_dim(row_part, offset, column_rows, 0)
        updated = present + owner_flag * column_total.reshape(column_rows, width_vecs)
        row_part = lax.dynamic_update_slice_in_dim(row_part, updated, offset, 0)
        return lax.psum_scatter(row_part, "col", scatter_dimension=0, tiled=True)

    current_vec = (apply_hamiltonian(vectors) - center * vectors) / halfwidth
    image = apply_hamiltonian(current_vec)
    following = 2.0 * (image - center * current_vec) / halfwidth - vectors
    current_vec = following
    gram_local = lax.dot_general(
        current_vec,
        current_vec,
        (((0,), (0,)), ((), ())),
        precision=lax.Precision.HIGHEST,
        preferred_element_type=jnp.float32,
    )
    gram_total = lax.psum(gram_local, ("row", "col"))
    return (current_vec, gram_total / total_rows)


def solution(mesh):
    in_specs = (
        P(("row", "col"), None, None),
        P(("row", "col")),
        P(("row", "col")),
        P(("row", "col")),
        P(),
        P(("row", "col"), None),
    )
    out_specs = (P(("row", "col"), None), P())
    return jax.shard_map(
        on_device, mesh=mesh, in_specs=in_specs, out_specs=out_specs, check_vma=False
    )
```

profile of v0, /device:TPU:1, one launch (start us, length us, event | category | flops | bytes accessed | tf_op | source)
XLA Modules:
  0.0 414.4 jit_solution(1064199134010569408)
XLA Ops:
  7.2 0.9 convert_element_type.16
  8.2 15.8 %all_gather.6 = bf16[1024,128]{1,0:T(8,128)(2,1)S(1)} all-gather(bf16[128,128]{1,0:T(8,128)(2,1)S(1)} %convert_element_type.16), channel_id=1, replica_groups=mesh['row'=4,'col'=8] {'col'}, dimensions={0}, use_global_device_ids=true | all-gather | bytes 294912 | tf_op jit(solution)/shard_map/all_gather | solution.py:35
  27.8 1.3 scatter_fusion.1
  29.9 37.0 %all-reduce.6.cloned.1.call-done = bf16[2,256,128]{2,1,0:T(8,128)(2,1)} async-done(((bf16[2,256,128]{2,1,0:T(8,128)(2,1)}), bf16[2,256,128]{2,1,0:T(8,128)(2,1)}) %all-reduce.6.cloned.1.call-update) | async-done | bytes 131088 | tf_op jit(solution)/shard_map/psum | solution.py:11
  66.9 1.5 gather_fusion
  68.5 1.7 convolution_bitcast_fusion.3
  70.2 1.5 copy.13
  71.8 1.3 scatter_fusion
  73.1 39.9 %all-reduce.8.cloned.1.call-done = f32[2,256,128]{2,1,0:T(8,128)} async-done(((f32[2,256,128]{2,1,0:T(8,128)}), f32[2,256,128]{2,1,0:T(8,128)}) %all-reduce.8.cloned.1.call-update) | async-done | bytes 262160 | tf_op jit(solution)/shard_map/psum | solution.py:50
  113.1 1.0 broadcast_multiply_fusion.1
  118.1 25.2 %reduce-scatter.3.cloned.1.call-done = f32[128,128]{1,0:T(8,128)} async-done(((f32[1024,128]{1,0:T(8,128)}), f32[128,128]{1,0:T(8,128)}) %reduce-scatter.3.cloned.1.call-update) | async-done | bytes 65552 | tf_op jit(solution)/shard_map/reduce_scatter | solution.py:55
  144.2 18.0 %all_gather.7 = bf16[1024,128]{1,0:T(8,128)(2,1)S(1)} all-gather(bf16[128,128]{1,0:T(8,128)(2,1)S(1)} %fusion.8), channel_id=1, replica_groups=mesh['row'=4,'col'=8] {'col'}, dimensions={0}, use_global_device_ids=true | all-gather | bytes 294912 | tf_op jit(solution)/shard_map/all_gather | solution.py:35
  164.4 1.3 scatter_fusion.3
  166.6 36.5 %all-reduce.10.cloned.1.call-done = bf16[2,256,128]{2,1,0:T(8,128)(2,1)} async-done(((bf16[2,256,128]{2,1,0:T(8,128)(2,1)}), bf16[2,256,128]{2,1,0:T(8,128)(2,1)}) %all-reduce.10.cloned.1.call-update) | async-done | bytes 131088 | tf_op jit(solution)/shard_map/psum | solution.py:11
  203.1 1.5 gather_fusion.2
  204.7 1.7 convolution_bitcast_fusion.1
  206.4 1.5 copy.17
  208.0 1.3 scatter_fusion.2
  209.3 39.5 %all-reduce.12.cloned.1.call-done = f32[2,256,128]{2,1,0:T(8,128)} async-done(((f32[2,256,128]{2,1,0:T(8,128)}), f32[2,256,128]{2,1,0:T(8,128)}) %all-reduce.12.cloned.1.call-update) | async-done | bytes 262160 | tf_op jit(solution)/shard_map/psum | solution.py:50
  248.8 1.0 broadcast_multiply_fusion
  250.7 28.2 %reduce-scatter.5.cloned.1.call-done = f32[128,128]{1,0:T(8,128)} async-done(((f32[1024,128]{1,0:T(8,128)}), f32[128,128]{1,0:T(8,128)}) %reduce-scatter.5.cloned.1.call-update) | async-done | bytes 65552 | tf_op jit(solution)/shard_map/reduce_scatter | solution.py:55
  279.8 0.9 fusion.10
  280.8 125.3 %all-reduce.14.cloned.1.call-done = f32[128,128]{1,0:T(8,128)} async-done(((f32[128,128]{1,0:T(8,128)}), f32[128,128]{1,0:T(8,128)}) %all-reduce.14.cloned.1.call-update) | async-done | bytes 65552 | tf_op jit(solution)/shard_map/psum | solution.py:68
  406.1 1.5 broadcast_multiply_fusion.2
  (58 shorter events, 11.0 us)
Async XLA Ops:
  7.2 19.5 %copy-start = (bf16[8,256,256]{2,1,0:T(8,128)(2,1)S(1)}, bf16[8,256,256]{2,1,0:T(8,128)(2,1)}, u32[]{:S(2)}) copy-start(bf16[8,256,256]{2,1,0:T(8,128)(2,1)} %param.6) | copy-start | bytes 3145732
  7.2 59.8 %all-reduce.6.cloned.1.call-start = ((), (), s32[]{:S(2)}) async-start(), calls=%async_computation.2 | async-start | bytes 262144 | tf_op jit(solution)/shard_map/psum | solution.py:11
  24.6 88.4 %all-reduce.8.cloned.1.call-start = ((), (), s32[]{:S(2)}) async-start(), calls=%async_computation.3 | async-start | bytes 524288 | tf_op jit(solution)/shard_map/psum | solution.py:50
  25.3 0.7 copy-start.9
  27.1 0.7 copy-start.10
  29.1 0.7 copy-start.4
  29.8 113.5 %reduce-scatter.3.cloned.1.call-start = ((), (), s32[]{:S(2)}) async-start(), calls=%async_computation.4 | async-start | bytes 589824 | tf_op jit(solution)/shard_map/reduce_scatter | solution.py:55
  114.1 0.8 copy-start.2
  114.1 0.9 copy-start.8
  114.1 29.3 %copy-start.5 = (f32[128,128]{1,0:T(8,128)S(1)}, f32[128,128]{1,0:T(8,128)}, u32[]{:S(2)}) copy-start(f32[128,128]{1,0:T(8,128)} %param.11) | copy-start | bytes 196612
  114.9 88.2 %all-reduce.10.cloned.1.call-start = ((), (), s32[]{:S(2)}) async-start(), calls=%async_computation.5 | async-start | bytes 262144 | tf_op jit(solution)/shard_map/psum | solution.py:11
  163.6 85.2 %all-reduce.12.cloned.1.call-start = ((), (), s32[]{:S(2)}) async-start(), calls=%async_computation.6 | async-start | bytes 524288 | tf_op jit(solution)/shard_map/psum | solution.py:50
  165.8 0.7 copy-start.3
  166.5 112.4 %reduce-scatter.5.cloned.1.call-start = ((), (), s32[]{:S(2)}) async-start(), calls=%async_computation.7 | async-start | bytes 589824 | tf_op jit(solution)/shard_map/reduce_scatter | solution.py:55
  249.9 0.8 copy-start.1
  249.9 29.1 %copy-start.7 = (f32[128,128]{1,0:T(8,128)S(1)}, f32[128,128]{1,0:T(8,128)}, u32[]{:S(2)}) copy-start(f32[128,128]{1,0:T(8,128)} %reduce-scatter.3.cloned.1.call-done) | copy-start | bytes 196612
  250.7 155.4 %all-reduce.14.cloned.1.call-start = ((), (), s32[]{:S(2)}) async-start(), calls=%async_computation.8 | async-start | bytes 131072 | tf_op jit(solution)/shard_map/psum | solution.py:68
  279.8 0.9 copy-start.6
Sparse Core Ops, SparseCore 0:
  24.8 42.1 all-reduce.5
  70.1 42.8 all-reduce.7
  115.3 28.0 reduce-scatter.2
  163.7 39.3 all-reduce.9
  205.9 42.9 all-reduce.11
  251.0 27.8 reduce-scatter.4
  285.1 120.9 all-reduce.13
where the time goes:
time: 415 us; the launch traced here: 414 us
  waiting for transfers between devices  332 us (80%)
  blocking collectives  33.8 us (8%)
  between operations  17.7 us (4%)
  local copies, waits for them, and re-layouts  12.8 us (3%)
  other arithmetic  12.8 us (3%)
  matrix products  5.15 us (1%)
    psum x1, waiting for transfers between devices, on_device(): gram_total = lax.psum(gram_local, ('row', 'col'))  125 us
    psum x2, waiting for transfers between devices, apply_hamiltonian(): column_total = lax.psum(col_part, 'row')  79.5 us
    psum x2, waiting for transfers between devices, spread(): return lax.psum(block, axis)  73.6 us
    reduce_scatter x2, waiting for transfers between devices, apply_hamiltonian(): return lax.psum_scatter(row_part, 'col', scatter_dimension=0, tiled=True)  53.5 us
    all_gather x2, blocking collectives, apply_hamiltonian(): row_panel = lax.all_gather(vector_panel, 'col', axis=0, tiled=True)  33.8 us
  transfers between devices with their start and end apart: 7, of which 7 were waited for; matrix products, arithmetic and copies ran while one was open for 4% of the time, Pallas kernels for 0%

commit v1 on v0

--- a/solution.py
+++ b/solution.py
@@ -8,7 +8,7 @@
 
 def spread(block, axis, holder):
     block = jnp.where(lax.axis_index(axis) == holder, block, jnp.zeros_like(block))
-    return lax.psum(block, axis)
+    return lax.all_gather(block, axis_name=axis).sum(axis=0)
 
 
 def on_device(tiles, tile_rows, tile_cols, tile_count, bounds, vectors):

time: 415 us -> 343 us (0.83)
  waiting for transfers between devices: 332 us -> 243 us
  blocking collectives: 33.8 us -> 54.1 us
    psum x2 -> x0, waiting for transfers between devices: 73.6 us -> none  [spread(): return lax.psum(block, axis)]
    all_gather x0 -> x2, blocking collectives: none -> 20 us  [spread(): return lax.all_gather(block, axis_name=axis).sum(axis=0)]
    psum x2, waiting for transfers between devices: 79.5 us -> 64 us  [apply_hamiltonian(): column_total = lax.psum(col_part, 'row')]
  transfers between devices with their start and end apart: 7 -> 5, of which waited for: 7 -> 5; matrix products, arithmetic and copies ran while one was open for 4% -> 3% of each run, Pallas kernels for 0% -> 0%
where the time goes in v1:
time: 343 us
  waiting for transfers between devices  243 us (71%)
  blocking collectives  54.1 us (16%)
  between operations  17.4 us (5%)
  other arithmetic  11.7 us (3%)
  local copies, waits for them, and re-layouts  11.6 us (3%)
  matrix products  5.16 us (2%)
    psum x1, waiting for transfers between devices, on_device(): gram_total = lax.psum(gram_local, ('row', 'col'))  125 us
    psum x2, waiting for transfers between devices, apply_hamiltonian(): column_total = lax.psum(col_part, 'row')  64 us
    reduce_scatter x2, waiting for transfers between devices, apply_hamiltonian(): return lax.psum_scatter(row_part, 'col', scatter_dimension=0, tiled=True)  53.4 us
    all_gather x2, blocking collectives, apply_hamiltonian(): row_panel = lax.all_gather(vector_panel, 'col', axis=0, tiled=True)  34.1 us
    all_gather x2, blocking collectives, spread(): return lax.all_gather(block, axis_name=axis).sum(axis=0)  20 us
  transfers between devices with their start and end apart: 5, of which 5 were waited for; matrix products, arithmetic and copies ran while one was open for 3% of the time, Pallas kernels for 0%

profile of v1, /device:TPU:1, one launch (start us, length us, event | category | flops | bytes accessed | tf_op | source)
XLA Modules:
  0.0 342.7 jit_solution(13657085534069359991)
XLA Ops:
  7.2 0.9 convert_element_type.20
  8.2 15.9 %all_gather.18 = bf16[1024,128]{1,0:T(8,128)(2,1)S(1)} all-gather(bf16[128,128]{1,0:T(8,128)(2,1)S(1)} %convert_element_type.20), channel_id=1, replica_groups=mesh['row'=4,'col'=8] {'col'}, dimensions={0}, use_global_device_ids=true | all-gather | bytes 294912 | tf_op jit(solution)/shard_map/all_gather | solution.py:35
  26.8 1.3 scatter_fusion.1
  29.2 11.0 %all-gather = bf16[2048,128]{1,0:T(8,128)(2,1)S(1)} all-gather(bf16[512,128]{1,0:T(8,128)(2,1)S(1)} %dynamic-slice_select_fusion.1), channel_id=2, replica_groups=mesh['row'=4,'col'=8] {'row'}, dimensions={0}, use_global_device_ids=true | all-gather | bytes 655360 | tf_op jit(solution)/shard_map/all_gather | solution.py:11
  41.0 1.7 convolution_bitcast_fusion.3
  42.7 1.5 copy.13
  44.3 1.3 scatter_fusion
  45.6 27.9 %all-reduce.4.cloned.1.call-done = f32[2,256,128]{2,1,0:T(8,128)} async-done(((f32[2,256,128]{2,1,0:T(8,128)}), f32[2,256,128]{2,1,0:T(8,128)}) %all-reduce.4.cloned.1.call-update) | async-done | bytes 262160 | tf_op jit(solution)/shard_map/psum | solution.py:50
  73.5 1.0 broadcast_multiply_fusion.1
  78.5 25.2 %reduce-scatter.3.cloned.1.call-done = f32[128,128]{1,0:T(8,128)} async-done(((f32[1024,128]{1,0:T(8,128)}), f32[128,128]{1,0:T(8,128)}) %reduce-scatter.3.cloned.1.call-update) | async-done | bytes 65552 | tf_op jit(solution)/shard_map/reduce_scatter | solution.py:55
  104.6 18.2 %all_gather.21 = bf16[1024,128]{1,0:T(8,128)(2,1)S(1)} all-gather(bf16[128,128]{1,0:T(8,128)(2,1)S(1)} %fusion.8), channel_id=1, replica_groups=mesh['row'=4,'col'=8] {'col'}, dimensions={0}, use_global_device_ids=true | all-gather | bytes 294912 | tf_op jit(solution)/shard_map/all_gather | solution.py:35
  122.8 9.0 %all-gather.1 = bf16[2048,128]{1,0:T(8,128)(2,1)S(1)} all-gather(bf16[512,128]{1,0:T(8,128)(2,1)S(1)} %dynamic-slice_select_fusion), channel_id=3, replica_groups=mesh['row'=4,'col'=8] {'row'}, dimensions={0}, use_global_device_ids=true | all-gather | bytes 655360 | tf_op jit(solution)/shard_map/all_gather | solution.py:11
  131.9 1.4 gather_fusion.2
  134.7 1.3 scatter_fusion.3
  136.8 1.7 convolution_bitcast_fusion.1
  138.5 1.5 copy.17
  140.1 1.3 scatter_fusion.2
  141.5 36.1 %all-reduce.6.cloned.1.call-done = f32[2,256,128]{2,1,0:T(8,128)} async-done(((f32[2,256,128]{2,1,0:T(8,128)}), f32[2,256,128]{2,1,0:T(8,128)}) %all-reduce.6.cloned.1.call-update) | async-done | bytes 262160 | tf_op jit(solution)/shard_map/psum | solution.py:50
  177.6 1.0 broadcast_multiply_fusion
  179.5 28.2 %reduce-scatter.5.cloned.1.call-done = f32[128,128]{1,0:T(8,128)} async-done(((f32[1024,128]{1,0:T(8,128)}), f32[128,128]{1,0:T(8,128)}) %reduce-scatter.5.cloned.1.call-update) | async-done | bytes 65552 | tf_op jit(solution)/shard_map/reduce_scatter | solution.py:55
  207.7 0.9 divide_subtract_fusion
  208.6 0.9 fusion.10
  209.5 125.1 %all-reduce.8.cloned.1.call-done = f32[128,128]{1,0:T(8,128)} async-done(((f32[128,128]{1,0:T(8,128)}), f32[128,128]{1,0:T(8,128)}) %all-reduce.8.cloned.1.call-update) | async-done | bytes 65552 | tf_op jit(solution)/shard_map/psum | solution.py:68
  334.7 1.5 broadcast_multiply_fusion.2
  (62 shorter events, 9.4 us)
Async XLA Ops:
  7.2 18.9 %copy-start = (bf16[8,256,256]{2,1,0:T(8,128)(2,1)S(1)}, bf16[8,256,256]{2,1,0:T(8,128)(2,1)}, u32[]{:S(2)}) copy-start(bf16[8,256,256]{2,1,0:T(8,128)(2,1)} %param.6) | copy-start | bytes 3145732
  7.2 66.3 %all-reduce.4.cloned.1.call-start = ((), (), s32[]{:S(2)}) async-start(), calls=%async_computation.2 | async-start | bytes 524288 | tf_op jit(solution)/shard_map/psum | solution.py:50
  8.1 15.9 %copy-start.12 = (s32[8]{0:T(128)S(1)}, s32[8]{0:T(128)}, u32[]{:S(2)}) copy-start(s32[8]{0:T(128)} %param.8) | copy-start | bytes 100
  24.0 2.0 copy-start.5
  24.7 0.7 copy-start.13
  28.1 0.7 copy-start.4
  28.2 1.0 copy-start.6
  28.9 74.8 %reduce-scatter.3.cloned.1.call-start = ((), (), s32[]{:S(2)}) async-start(), calls=%async_computation.3 | async-start | bytes 589824 | tf_op jit(solution)/shard_map/reduce_scatter | solution.py:55
  74.5 0.8 copy-start.2
  74.5 0.9 copy-start.11
  74.5 29.2 %copy-start.8 = (f32[128,128]{1,0:T(8,128)S(1)}, f32[128,128]{1,0:T(8,128)}, u32[]{:S(2)}) copy-start(f32[128,128]{1,0:T(8,128)} %param.11) | copy-start | bytes 196612
  75.3 102.3 %all-reduce.6.cloned.1.call-start = ((), (), s32[]{:S(2)}) async-start(), calls=%async_computation.4 | async-start | bytes 524288 | tf_op jit(solution)/shard_map/psum | solution.py:50
  134.7 2.1 copy-start.7
  136.0 0.7 copy-start.3
  136.8 70.9 %reduce-scatter.5.cloned.1.call-start = ((), (), s32[]{:S(2)}) async-start(), calls=%async_computation.5 | async-start | bytes 589824 | tf_op jit(solution)/shard_map/reduce_scatter | solution.py:55
  178.6 0.8 copy-start.1
  178.6 29.1 %copy-start.10 = (f32[128,128]{1,0:T(8,128)S(1)}, f32[128,128]{1,0:T(8,128)}, u32[]{:S(2)}) copy-start(f32[128,128]{1,0:T(8,128)} %reduce-scatter.3.cloned.1.call-done) | copy-start | bytes 196612
  179.4 155.2 %all-reduce.8.cloned.1.call-start = ((), (), s32[]{:S(2)}) async-start(), calls=%async_computation.6 | async-start | bytes 131072 | tf_op jit(solution)/shard_map/psum | solution.py:68
  208.6 0.9 copy-start.9
Sparse Core Ops, SparseCore 0:
  29.0 44.4 all-reduce.3
  75.8 27.8 reduce-scatter.2
  136.9 40.6 all-reduce.5
  179.8 27.8 reduce-scatter.4
  213.7 120.9 all-reduce.7
